TPU v7x, 32 devices: a whole 2x2x4 slice. The times are simulated.
32 devices in a mesh: sp: 8 (over y, x, core), dp: 4 (over z).
Axes of the slice: x: 2, y: 2, z: 4, core: 2. Of those that a mesh axis runs over, the one named last changes fastest.
Arguments:
- hidden: bfloat16 [4, 2048, 4096], P('dp', 'sp'), may hold values from -24 to 24
- pad_counts: int32 [4, 8], P('dp', 'sp'), may hold values from 64 to 128
- doc_lengths: int32 [4, 32], P('dp'), may hold values from 1 to 128, 2048 in all within a row
- range_shift: int32 [4, 8], P('dp'), may hold values from -32 to 32
- qkv_weight: bfloat16 [4096, 384], P('dp'), may hold values from -0.09375 to 0.09375
Outputs:
- attended: bfloat16 [4, 2048, 128], P('dp', 'sp')
Inputs may be any that keep to these rules, and one draw needn't show every extreme that they name: `doc_lengths`: each row sums to 2048.
All inputs are finite; a program needn't handle non-finite values.
Results may differ from a plain program's by a relative error of at most 0.0095.
Values may be sent and summed in bfloat16 or wider, within the bound.
A program may use at most 64 MiB of HBM per device.

v0:
```python
import math

import jax
import jax.numpy as jnp
from jax import lax
from jax.sharding import PartitionSpec as P


def carried_in(value, axis, combine, identity):
    devices, index = (lax.axis_size(axis), lax.axis_index(axis))
    everything = lax.all_gather(value, axis)
    start = jnp.broadcast_to(jnp.asarray(identity, value.dtype), value.shape)

    def hop(k, before):
        reached = k < index
        new = combine(before, everything[k])
        return jnp.where(reached, new, before)

    return lax.fori_loop(0, devices, hop, start)


def extended_2(cells, sides, width):
    for axis, dim in sides:
        count = lax.axis_size(axis)
        ends = count - 1
        head = lax.slice_in_dim(cells, 0, width, axis=dim)
        tail = lax.slice_in_dim(cells, cells.shape[dim] - width, cells.shape[dim], axis=dim)
        cells = jnp.concatenate(
            [
                lax.ppermute(tail, axis, [(i, (i + 1) % count) for i in range(ends)]),
                cells,
                lax.ppermute(head, axis, [((i + 1) % count, i) for i in range(ends)]),
            ],
            axis=dim,
        )
    return cells


def add_counts(earlier, later):
    return earlier + later


def edge_slots(rows, padding, edge_count):
    total_rows = rows.shape[0]
    return jnp.concatenate(
        [lax.dynamic_slice_in_dim(rows, padding, edge_count, 0), rows[total_rows - edge_count :]],
        axis=0,
    )


def with_edges(rows, extended, edge_count):
    return jnp.concatenate([extended[:edge_count], rows, extended[3 * edge_count :]], axis=0)


def project(inputs, qkv_weight):
    summed = jnp.dot(
        inputs,
        lax.all_gather(qkv_weight, "dp", axis=0, tiled=True),
        preferred_element_type=jnp.float32,
    )
    return summed.astype(jnp.bfloat16)


def shards(hidden, pad_counts, doc_lengths, range_shift, qkv_weight):
    slot_rows = hidden[0]
    rows_dev = slot_rows.shape[0]
    edge_count = rows_dev // 8
    padding = pad_counts[0, 0]
    live_count = rows_dev - padding
    token_start = carried_in(live_count, "sp", add_counts, jnp.int32(0))
    axis_size = lax.axis_size("sp")
    device_index = lax.axis_index("sp")
    shifts = range_shift[0]
    range_first = jnp.where(
        device_index == 0, 0, token_start + jnp.take(shifts, device_index)
    ).astype(jnp.int32)
    next_shift = jnp.take(shifts, jnp.minimum(device_index + 1, axis_size - 1))
    range_end = jnp.where(
        device_index == axis_size - 1,
        token_start + live_count,
        token_start + live_count + next_shift,
    ).astype(jnp.int32)
    owned_count = range_end - range_first
    local_rows = jnp.arange(rows_dev, dtype=jnp.int32)
    position = range_first + local_rows
    row_live = local_rows < owned_count
    source = position - token_start + edge_count + jnp.where(position >= token_start, padding, 0)
    source = jnp.clip(source, 0, rows_dev + 2 * edge_count - 1)
    extended = extended_2(edge_slots(slot_rows, padding, edge_count), (("sp", 0),), edge_count)
    candidates = with_edges(slot_rows, extended, edge_count)
    owned_rows = jnp.where(row_live[:, None], jnp.take(candidates, source, axis=0), 0)
    projected = project(owned_rows, qkv_weight)
    head_dim = projected.shape[1] // 3
    query = projected[:, :head_dim]
    keys = projected[:, head_dim : 2 * head_dim]
    values = projected[:, 2 * head_dim :]
    doc_ends = jnp.cumsum(doc_lengths[0])
    doc_ids = jnp.sum((doc_ends[None, :] <= position[:, None]).astype(jnp.int32), axis=1)
    scores = jnp.einsum("qd,kd->qk", query, keys, preferred_element_type=jnp.float32) / math.sqrt(
        head_dim
    )
    allowed = (doc_ids[:, None] == doc_ids[None, :]) & (position[None, :] <= position[:, None])
    allowed = allowed & row_live[:, None] & row_live[None, :]
    masked = jnp.where(allowed, scores, -1e30)
    row_peak = jnp.max(masked, axis=1, keepdims=True)
    exponent = jnp.where(allowed, jnp.exp(masked - row_peak), 0.0)
    denominator = jnp.sum(exponent, axis=1, keepdims=True)
    attention_probs = (exponent / jnp.where(row_live[:, None], denominator, 1.0)).astype(
        jnp.bfloat16
    )
    result = jnp.dot(attention_probs, values, preferred_element_type=jnp.float32)
    attended = jnp.where(row_live[:, None], result, 0.0).astype(jnp.bfloat16)
    return attended[None]


def solution(mesh):
    in_specs = (P("dp", "sp", None), P("dp", "sp"), P("dp", None), P("dp", None), P("dp", None))
    out_specs = P("dp", "sp", None)
    return jax.shard_map(shards, mesh=mesh, in_specs=in_specs, out_specs=out_specs, check_vma=False)
```

profile of v0, /device:TPU:0, one launch (start us, length us, event | category | flops | bytes accessed | tf_op | source)
XLA Modules:
  0.0 87.3 jit_solution(15151462014178972932)
XLA Ops:
  6.5 0.7 all-gather.2.cloned.1.call-update
  7.9 1.1 %slice_bitcast_fusion = (bf16[32,4096]{1,0:T(8,128)(2,1)S(1)}, bf16[32,4096]{1,0:T(8,128)(2,1)S(1)}) fusion(bf16[1,256,4096]{2,1,0:T(8,128)(2,1)} %param.7, s32[]{:T(128)S(6)} %select_n.104), kind=kLoop, calls=%fused_computation.18 | loop fusion | bytes 1048580 | tf_op jit(solution)/shard_map/slice | solution.py:46
  9.0 2.4 %collective-permute-start = (bf16[32,4096]{1,0:T(8,128)(2,1)S(1)}, bf16[32,4096]{1,0:T(8,128)(2,1)S(1)}, u32[]{:S(2)}, u32[]{:S(2)}) collective-permute-start(bf16[32,4096]{1,0:T(8,128)(2,1)S(1)} %get-tuple-element.115), channel_id=1, source_target_pairs={{0,4},{4,8},{8,12},{12,16},{16,20},{20,24},{24,28},{1,5},{5,9},{9,... | collective-permute-start | bytes 786440 | tf_op jit(solution)/shard_map/ppermute | solution.py:30
  11.4 1.3 %dynamic-slice.9 = u32[1]{0:T(128)} dynamic-slice(u32[32]{0:T(128)} %constant.142, u32[]{:T(128)S(6)} %add.156), dynamic_slice_sizes={1} | dynamic-slice | bytes 12
  12.7 0.7 dynamic-update-slice.2
  13.4 1.3 %collective-permute-start.1 = (bf16[32,4096]{1,0:T(8,128)(2,1)S(1)}, bf16[32,4096]{1,0:T(8,128)(2,1)S(1)}, u32[]{:S(2)}, u32[]{:S(2)}) collective-permute-start(bf16[32,4096]{1,0:T(8,128)(2,1)S(1)} %get-tuple-element.116), channel_id=1, source_target_pairs={{4,0},{8,4},{12,8},{16,12},{20,16},{24,20},{28,24},{5,1},{9,5},{13... | collective-permute-start | bytes 786440 | tf_op jit(solution)/shard_map/ppermute | solution.py:32
  14.7 12.4 %all-reduce = s32[8]{0:T(128)S(1)} all-reduce(s32[8]{0:T(128)S(1)} %dynamic-update-slice.2), channel_id=1, replica_groups=mesh['sp'=8,'dp'=4] {'sp'}, use_global_device_ids=true, to_apply=%add | all-reduce | flops 8 | bytes 64
  27.1 11.1 %while.15 = (s32[]{:T(128)}, s32[]{:T(128)}, s32[]{:T(128)}, s32[8]{0:T(128)S(1)}, s32[]{:T(128)}) while((s32[]{:T(128)}, s32[]{:T(128)}, s32[]{:T(128)}, s32[8]{0:T(128)S(1)}, s32[]{:T(128)}) %tuple.42), condition=%wide.region_1.2_spmd, body=%wide.region_0.1_spmd.sunk | while | flops 5 | bytes 107 | solution.py:19
  27.1 0.7 dynamic_slice.16
  28.4 0.7 dynamic_slice.16
  29.8 0.7 dynamic_slice.16
  31.2 0.7 dynamic_slice.16
  32.6 0.7 dynamic_slice.16
  34.0 0.7 dynamic_slice.16
  35.4 0.7 dynamic_slice.16
  36.8 0.7 dynamic_slice.16
  38.1 1.4 %constant_dynamic-slice_fusion.1 = (s32[1,1]{1,0:T(1,128)}, s32[1,1]{1,0:T(1,128)}) fusion(s32[1,8]{1,0:T(1,128)} %param.10, s32[]{:T(128)S(6)} %select_n.96, s32[]{:T(128)S(6)} %select_n.99), kind=kLoop, calls=%fused_computation.37 | loop fusion | bytes 24 | solution.py:77
  40.9 0.7 copy.8
  41.9 1.8 %pad_maximum_fusion = bf16[320,4096]{1,0:T(8,128)(2,1)S(1)} fusion(bf16[32,4096]{1,0:T(8,128)(2,1)S(1)} %collective-permute-done.1, bf16[256,4096]{1,0:T(8,128)(2,1)} %bitcast.28, bf16[32,4096]{1,0:T(8,128)(2,1)S(1)} %collective-permute-done), kind=kLoop, calls=%fused_computation.1 | loop fusion | flops 7864320 | bytes 5242880 | tf_op jit(solution)/shard_map/concatenate | solution.py:52
  43.7 3.2 %gather_fusion = bf16[256,4096]{1,0:T(8,128)(2,1)} fusion(bf16[320,4096]{1,0:T(8,128)(2,1)S(1)} %pad_maximum_fusion, s32[1024]{0:T(1024)S(1)} %pad_clamp_fusion), kind=kCustom, calls=%fused_computation | custom fusion | bytes 4195328 | tf_op jit(solution)/shard_map/jit(_take)/gather | solution.py:91
  46.9 28.3 %all-gather.2.cloned.1.call-done = bf16[4096,384]{1,0:T(8,128)(2,1)} async-done(((bf16[1024,384]{1,0:T(8,128)(2,1)}), bf16[4096,384]{1,0:T(8,128)(2,1)}) %all-gather.2.cloned.1.call-update) | async-done | bytes 3145744 | tf_op jit(solution)/shard_map/all_gather | solution.py:58
  75.2 3.8 %fusion.5 = bf16[256,384]{1,0:T(8,128)(2,1)S(1)} fusion(bf16[4096,384]{1,0:T(8,128)(2,1)} %all-gather.2.cloned.1.call-done, bf16[256,4096]{1,0:T(8,128)(2,1)} %gather_fusion, pred[256]{0:T(512)(128)(4,1)S(1)} %get-tuple-element.121, pred[256]{0:T(512)(128)(4,1)S(1)} %get-tuple-element.122), kind=kOutput, calls=%fused_computation.7 | convolution fusion | flops 807501824 | bytes 5440000 | tf_op jit(solution)/shard_map/dot_general | solution.py:56
  79.0 0.2 fusion.23
  79.4 1.0 %fusion.10 = bf16[1,256,128]{2,1,0:T(8,128)(2,1)} fusion(f32[256,256]{0,1:T(8,128)S(1)} %get-tuple-element.120, f32[256]{0:T(256)S(1)} %broadcast_select_fusion, f32[256]{0:T(256)S(1)} %get-tuple-element.119, bf16[256,384]{1,0:T(8,128)(2,1)S(1)} %fusion.5, pred[256]{0:T(512)(128)(4,1)S(1)} %get-tuple-element.122, s32[256]{0:T(256)S(1)} %iota_add_fusion, ...), kind=kOutput, calls=%fused_computation.12 | convolution fusion | flops 17432576 | bytes 400896 | tf_op jit(solution)/shard_map/dot_general | solution.py:111
  (13 shorter events, 0.5 us)
Async XLA Ops:
  6.5 68.6 %all-gather.2.cloned.1.call-start = ((), (), s32[]{:S(2)}) async-start(), calls=%async_computation | async-start | bytes 3932160 | tf_op jit(solution)/shard_map/all_gather | solution.py:58
  9.0 32.8 %collective-permute-start = (bf16[32,4096]{1,0:T(8,128)(2,1)S(1)}, bf16[32,4096]{1,0:T(8,128)(2,1)S(1)}, u32[]{:S(2)}, u32[]{:S(2)}) collective-permute-start(bf16[32,4096]{1,0:T(8,128)(2,1)S(1)} %get-tuple-element.115), channel_id=1, source_target_pairs={{0,4},{4,8},{8,12},{12,16},{16,20},{20,24},{24,28},{1,5},{5,9},{9,... | collective-permute-start | bytes 786440 | tf_op jit(solution)/shard_map/ppermute | solution.py:30
  13.4 28.5 %collective-permute-start.1 = (bf16[32,4096]{1,0:T(8,128)(2,1)S(1)}, bf16[32,4096]{1,0:T(8,128)(2,1)S(1)}, u32[]{:S(2)}, u32[]{:S(2)}) collective-permute-start(bf16[32,4096]{1,0:T(8,128)(2,1)S(1)} %get-tuple-element.116), channel_id=1, source_target_pairs={{4,0},{8,4},{12,8},{16,12},{20,16},{24,20},{28,24},{5,1},{9,5},{13... | collective-permute-start | bytes 786440 | tf_op jit(solution)/shard_map/ppermute | solution.py:32
Sparse Core Ops, SparseCore 0:
  8.9 66.1 all-gather.1
where the time goes:
time: 87.6 us; the launch traced here: 87.3 us
  waiting for transfers between devices  29 us (33%)
  between operations  15.4 us (18%)
  local copies, waits for them, and re-layouts  13.8 us (16%)
  blocking collectives  12.4 us (14%)
  loops' own time  5.72 us (7%)
  matrix products  5.07 us (6%)
  starting transfers between devices  3.66 us (4%)
  other arithmetic  2.28 us (3%)
    all_gather x1, waiting for transfers between devices, project(): lax.all_gather(qkv_weight, 'dp', axis=0, tiled=True)  28.3 us
    unnamed x1, blocking collectives  12.4 us
    another operation x1, loops' own time, carried_in(): return lax.fori_loop(0, devices, hop, start)  5.72 us
    dynamic_slice x8, local copies, waits for them, and re-layouts, hop(): new = combine(before, everything[k])  5.35 us
    dot_general x1, matrix products, project(): jnp.dot(inputs, lax.all_gather(qkv_weight, 'dp', axis=0, tiled=True), pre...  3.83 us
    gather x1, local copies, waits for them, and re-layouts, shards(): jnp.take(candidates, source, axis=0)  3.22 us
    ppermute x1, starting transfers between devices, extended_2(): lax.ppermute(tail, axis, [(i, (i + 1) % count) for i in range(ends)])  2.37 us
    unnamed x3, local copies, waits for them, and re-layouts  1.98 us
  transfers between devices with their start and end apart: 3, of which 1 were waited for; matrix products, arithmetic and copies ran while one was open for 18% of the time, Pallas kernels for 0%

commit v1 on v0

v1 whole, which is shorter than its diff:
```python
import functools
import math

import jax
import jax.numpy as jnp
from jax import lax
from jax.experimental import pallas as pl
from jax.experimental.pallas import tpu as pltpu
from jax.sharding import PartitionSpec as P

MESH = pl.DeviceIdType.MESH


def flipped(index, bits):
    out, bit = index, 1
    while bit <= bits:
        if bits & bit:
            out = out + bit - 2 * bit * ((index // bit) % 2)
        bit *= 2
    return out


def share_count(chips, depth):
    for shares in (4, 2):
        halves = 2 if shares == 4 else 1
        if chips % shares == 0 and depth % (2 * shares * halves * 16) == 0:
            return shares
    return 1


def kernel(
    n_sp,
    n_dp,
    shares,
    hidden_ref,
    pad_ref,
    docs_ref,
    shift_ref,
    weight_ref,
    out_ref,
    rows_buf,
    weights,
    total,
    pads,
    cand,
    head,
    local_sem,
    z_send,
    z_recv,
    plane_send,
    plane_recv,
    diag_send,
    diag_recv,
    sib_send,
    sib_recv,
    pad_send,
    pad_recv,
    edge_send,
    edge_recv,
):
    sp, dp = lax.axis_index("sp"), lax.axis_index("dp")
    rows_dev = hidden_ref.shape[1]
    depth, columns = weight_ref.shape
    head_dim = columns // 3
    least_pad = rows_dev // 4
    slots = rows_dev - least_pad
    edge = rows_dev // 8
    core = sp % 2
    place = (sp // 2) % shares
    sibling = flipped(sp, 1)
    piece = depth // (2 * shares)
    over_x, over_y, over_xy = flipped(place, 1), flipped(place, 2), flipped(place, 3)
    x_peer, y_peer = flipped(sp, 2), flipped(sp, 4)
    shards = [flipped(dp, j) for j in range(1, n_dp)]
    prior, later = (sp + n_sp - 1) % n_sp, (sp + 1) % n_sp

    def rows_of(which_core, which_place, half=None):
        start = (which_core * shares + which_place) * piece
        if half is None:
            return pl.ds(pl.multiple_of(start, 16), piece)
        return pl.ds(pl.multiple_of(start + half * (piece // 2), 16), piece // 2)

    fetch_rows = pltpu.make_async_copy(
        hidden_ref.at[0, pl.ds(least_pad, slots), :], rows_buf, local_sem.at[0]
    )
    fetch_rows.start()
    fetch_weight = pltpu.make_async_copy(weight_ref, weights.at[dp], local_sem.at[1])
    fetch_weight.start()
    padding = pad_ref[0, 0]
    pads[sp] = jnp.full(pads.shape[1:], padding, jnp.int32)

    barrier = pltpu.get_barrier_semaphore()
    for j in range(1, n_sp):
        pl.semaphore_signal(
            barrier, inc=1, device_id={"sp": (sp + j) % n_sp}, device_id_type=MESH
        )
    for j in range(1, n_dp):
        pl.semaphore_signal(
            barrier, inc=1, device_id={"dp": shards[j - 1]}, device_id_type=MESH
        )
    pl.semaphore_wait(barrier, n_sp - 1 + n_dp - 1)

    started = []

    def send(src, dst, send_sem, recv_sem, device):
        copy = pltpu.make_async_remote_copy(
            src_ref=src,
            dst_ref=dst,
            send_sem=send_sem,
            recv_sem=recv_sem,
            device_id=device,
            device_id_type=MESH,
        )
        copy.start()
        started.append(copy)

    def arrived(dst, send_sem, recv_sem, device):
        pltpu.make_async_remote_copy(
            src_ref=dst,
            dst_ref=dst,
            send_sem=send_sem,
            recv_sem=recv_sem,
            device_id=device,
            device_id_type=MESH,
        ).wait_recv()

    own = rows_of(core, place)
    for j in range(n_dp - 1):
        send(
            weight_ref.at[own, :],
            weights.at[dp, own, :],
            z_send.at[j],
            z_recv.at[j],
            {"dp": shards[j]},
        )
    for j in range(1, n_sp):
        send(pads.at[sp], pads.at[sp], pad_send.at[j - 1], pad_recv.at[j - 1], {"sp": (sp + j) % n_sp})

    def to_sibling(j, slot, rows):
        block = weights.at[shards[j], rows, :]
        send(block, block, sib_send.at[j, slot], sib_recv.at[j, slot], {"sp": sibling})

    def from_plane(j):
        block = weights.at[shards[j], own, :]
        arrived(block, z_send.at[j], z_recv.at[j], {"dp": shards[j]})
        if shares >= 2:
            send(block, block, plane_send.at[j, 0], plane_recv.at[j, 0], {"sp": x_peer})
        if shares >= 4:
            send(block, block, plane_send.at[j, 1], plane_recv.at[j, 1], {"sp": y_peer})
        to_sibling(j, 0, own)

    def from_neighbours(j):
        if shares >= 2:
            rows = rows_of(core, over_x)
            arrived(weights.at[shards[j], rows, :], plane_send.at[j, 0], plane_recv.at[j, 0], {"sp": x_peer})
            if shares >= 4:
                block = weights.at[shards[j], rows_of(core, over_x, 0), :]
                send(block, block, diag_send.at[j, 0], diag_recv.at[j, 0], {"sp": y_peer})
            to_sibling(j, 1, rows)
        if shares >= 4:
            rows = rows_of(core, over_y)
            arrived(weights.at[shards[j], rows, :], plane_send.at[j, 1], plane_recv.at[j, 1], {"sp": y_peer})
            block = weights.at[shards[j], rows_of(core, over_y, 1), :]
            send(block, block, diag_send.at[j, 1], diag_recv.at[j, 1], {"sp": x_peer})
            to_sibling(j, 2, rows)

    def from_diagonal(j):
        if shares >= 4:
            for half, peer in ((0, y_peer), (1, x_peer)):
                block = weights.at[shards[j], rows_of(core, over_xy, half), :]
                arrived(block, diag_send.at[j, half], diag_recv.at[j, half], {"sp": peer})
            to_sibling(j, 3, rows_of(core, over_xy))

    def from_sibling(j):
        places = [place, over_x, over_y, over_xy][:shares]
        for slot, which in enumerate(places):
            block = weights.at[shards[j], rows_of(1 - core, which), :]
            arrived(block, sib_send.at[j, slot], sib_recv.at[j, slot], {"sp": sibling})

    def product(shard):
        part = pl.ds(pl.multiple_of(shard * depth, 128), depth)
        return jnp.dot(rows_buf[:, part], weights[shard], preferred_element_type=jnp.float32)

    def own_shard():
        fetch_rows.wait()
        fetch_weight.wait()
        total[...] = product(dp)

    own_shard()
    for j in range(n_dp - 1):
        from_plane(j)
        if j > 0:
            from_diagonal(j - 1)
        from_neighbours(j)
        if j > 0:
            from_sibling(j - 1)
            total[...] += product(shards[j - 1])

    for j in range(1, n_sp):
        block = pads.at[(sp + n_sp - j) % n_sp]
        arrived(block, pad_send.at[j - 1], pad_recv.at[j - 1], {"sp": (sp + j) % n_sp})
    before = jnp.zeros(pads.shape[1:], jnp.int32)
    for i in range(n_sp):
        before = before + jnp.where(i < sp, rows_dev - pads[i], 0)
    live = rows_dev - padding
    shift = jnp.where(sp == 0, 0, shift_ref[0, sp])
    next_shift = jnp.where(sp == n_sp - 1, 0, shift_ref[0, later])
    owned_count = live + next_shift - shift
    docs = docs_ref.shape[1]
    lengths = jnp.broadcast_to(docs_ref[...].astype(jnp.float32), (8, docs)).astype(jnp.bfloat16)
    upper = (
        lax.broadcasted_iota(jnp.int32, (docs, docs), 0)
        <= lax.broadcasted_iota(jnp.int32, (docs, docs), 1)
    ).astype(jnp.float32).astype(jnp.bfloat16)
    ends = jnp.dot(lengths, upper, preferred_element_type=jnp.float32)[0:1].astype(jnp.int32)
    row = lax.broadcasted_iota(jnp.int32, (rows_dev, rows_dev), 0)
    col = lax.broadcasted_iota(jnp.int32, (rows_dev, rows_dev), 1)
    doc_row = lax.broadcasted_iota(jnp.int32, (rows_dev, docs), 0)
    local_ends = jnp.broadcast_to(ends - before[0:1, 0:1] - shift, (rows_dev, docs))
    doc_start = jnp.max(
        jnp.where(local_ends <= doc_row, local_ends, -(before[0:1, 0:1] + shift)).astype(jnp.float32),
        axis=1,
        keepdims=True,
    )
    allowed = (col <= row) & (col.astype(jnp.float32) >= doc_start)
    moved = row + shift
    target = jnp.where(
        moved < 0, edge + moved, jnp.where(moved < live, padding + moved, edge + moved - live)
    )
    pick = ((col == target) & (row < owned_count)).astype(jnp.float32).astype(jnp.bfloat16)
    head_row = lax.broadcasted_iota(jnp.int32, (edge, slots), 0)
    head_col = lax.broadcasted_iota(jnp.int32, (edge, slots), 1)
    head_pick = (head_col == head_row + padding - least_pad).astype(jnp.float32).astype(jnp.bfloat16)
    query_live = lax.broadcasted_iota(jnp.int32, (rows_dev, head_dim), 0) < owned_count

    if n_dp > 1:
        from_diagonal(n_dp - 2)
        from_sibling(n_dp - 2)
        projected = (total[...] + product(shards[n_dp - 2])).astype(jnp.bfloat16)
    else:
        projected = total[...].astype(jnp.bfloat16)

    own_rows = pl.ds(2 * edge, slots)
    cand[own_rows, :] = projected
    tail = cand.at[pl.ds(rows_dev - edge, edge), :]
    send(tail, cand.at[pl.ds(0, edge), :], edge_send.at[0], edge_recv.at[0], {"sp": later})
    head[...] = jnp.dot(head_pick, projected, preferred_element_type=jnp.float32).astype(jnp.bfloat16)
    send(head, cand.at[pl.ds(edge, edge), :], edge_send.at[1], edge_recv.at[1], {"sp": prior})
    arrived(cand.at[pl.ds(0, edge), :], edge_send.at[0], edge_recv.at[0], {"sp": later})
    arrived(cand.at[pl.ds(edge, edge), :], edge_send.at[1], edge_recv.at[1], {"sp": prior})

    qkv = jnp.dot(pick, cand[...], preferred_element_type=jnp.float32).astype(jnp.bfloat16)
    query, keys, values = qkv[:, :head_dim], qkv[:, head_dim : 2 * head_dim], qkv[:, 2 * head_dim :]
    scores = lax.dot_general(
        query, keys, (((1,), (1,)), ((), ())), preferred_element_type=jnp.float32
    ) * (1.0 / math.sqrt(head_dim))
    masked = jnp.where(allowed, scores, -1e30)
    peak = jnp.max(masked, axis=1, keepdims=True)
    exponent = jnp.where(allowed, jnp.exp(masked - peak), 0.0)
    probs = (exponent / jnp.sum(exponent, axis=1, keepdims=True)).astype(jnp.bfloat16)
    result = jnp.dot(probs, values, preferred_element_type=jnp.float32)
    out_ref[0] = jnp.where(query_live, result, 0.0).astype(out_ref.dtype)
    for copy in started:
        copy.wait_send()


def solution(mesh):
    n_sp, n_dp = mesh.shape["sp"], mesh.shape["dp"]

    def step(hidden, pad_counts, doc_lengths, range_shift, qkv_weight):
        rows_dev, width = hidden.shape[1:]
        depth, columns = qkv_weight.shape
        shares = share_count(n_sp // 2, depth)
        edge, slots = rows_dev // 8, rows_dev - rows_dev // 4
        others = max(n_dp - 1, 1)
        dma = pltpu.SemaphoreType.DMA
        return pl.pallas_call(
            functools.partial(kernel, n_sp, n_dp, shares),
            out_shape=jax.ShapeDtypeStruct((1, rows_dev, columns // 3), hidden.dtype),
            in_specs=[
                pl.BlockSpec(memory_space=pl.ANY),
                pl.BlockSpec(memory_space=pltpu.SMEM),
                pl.BlockSpec(memory_space=pltpu.VMEM),
                pl.BlockSpec(memory_space=pltpu.SMEM),
                pl.BlockSpec(memory_space=pl.ANY),
            ],
            out_specs=pl.BlockSpec(memory_space=pltpu.VMEM),
            scratch_shapes=[
                pltpu.VMEM((slots, width), hidden.dtype),
                pltpu.VMEM((n_dp, depth, columns), qkv_weight.dtype),
                pltpu.VMEM((slots, columns), jnp.float32),
                pltpu.VMEM((n_sp, 8, 128), jnp.int32),
                pltpu.VMEM((rows_dev, columns), hidden.dtype),
                pltpu.VMEM((edge, columns), hidden.dtype),
                dma((2,)),
                dma((others,)),
                dma((others,)),
                dma((others, 2)),
                dma((others, 2)),
                dma((others, 2)),
                dma((others, 2)),
                dma((others, shares)),
                dma((others, shares)),
                dma((n_sp - 1,)),
                dma((n_sp - 1,)),
                dma((2,)),
                dma((2,)),
            ],
            compiler_params=pltpu.CompilerParams(
                collective_id=0, has_side_effects=True, vmem_limit_bytes=48 * 1024 * 1024
            ),
            cost_estimate=pl.CostEstimate(
                flops=2 * slots * width * columns,
                bytes_accessed=2 * width * (rows_dev + columns),
                transcendentals=rows_dev * rows_dev,
            ),
        )(hidden, pad_counts, doc_lengths, range_shift, qkv_weight)

    in_specs = (P("dp", "sp", None), P("dp", "sp"), P("dp", None), P("dp", None), P("dp", None))
    return jax.shard_map(
        step, mesh=mesh, in_specs=in_specs, out_specs=P("dp", "sp", None), check_vma=False
    )
```

time: 87.6 us -> 39.7 us (0.45)
  Pallas kernels: 0 us -> 34.1 us
  waiting for transfers between devices: 29 us -> 0 us
  between operations: 15.4 us -> 0.67 us
  blocking collectives: 12.4 us -> 0 us
  local copies, waits for them, and re-layouts: 13.8 us -> 4.66 us
  loops' own time: 5.72 us -> 0 us
  matrix products: 5.07 us -> 0 us
  starting transfers between devices: 3.66 us -> 0 us
  other arithmetic: 2.28 us -> 0 us
    pallas_call x0 -> x1, Pallas kernels: none -> 34.1 us  [step(): pl.pallas_call(functools.partial(kernel, n_sp, n_dp, shares), out_shape=j...]
    all_gather x1 -> x0, waiting for transfers between devices: 28.3 us -> none  [project(): lax.all_gather(qkv_weight, 'dp', axis=0, tiled=True)]
    unnamed x1 -> x0, blocking collectives: 12.4 us -> none
    another operation x1 -> x0, loops' own time: 5.72 us -> none  [carried_in(): return lax.fori_loop(0, devices, hop, start)]
    dynamic_slice x8 -> x0, local copies, waits for them, and re-layouts: 5.35 us -> none  [hop(): new = combine(before, everything[k])]
    dot_general x3 -> x0, matrix products: 5.07 us -> none  [the longest x1 3.83 us: project(): jnp.dot(inputs, lax.all_gather(qkv_weight, 'dp', axis=0, tiled=True), pre...]
    ppermute x2 -> x0, starting transfers between devices: 3.65 us -> none  [the longest x1 2.37 us: extended_2(): lax.ppermute(tail, axis, [(i, (i + 1) % count) for i in range(ends)])]
    gather x1 -> x0, local copies, waits for them, and re-layouts: 3.22 us -> none  [shards(): jnp.take(candidates, source, axis=0)]
  transfers between devices with their start and end apart: 3 -> 0, of which waited for: 1 -> 0; matrix products, arithmetic and copies ran while one was open for 18% -> 0% of each run, Pallas kernels for 0% -> 0%
where the time goes in v1:
time: 39.7 us; the launch traced here: 39.4 us
  Pallas kernels  34.1 us (86%)
  local copies, waits for them, and re-layouts  4.66 us (12%)
  between operations  0.67 us (2%)
    pallas_call x1, Pallas kernels, step(): pl.pallas_call(functools.partial(kernel, n_sp, n_dp, shares), out_shape=j...  34.1 us
    unnamed x9, local copies, waits for them, and re-layouts  4.66 us

profile of v1, /device:TPU:0, one launch (start us, length us, event | category | flops | bytes accessed | tf_op | source)
XLA Modules:
  0.0 39.4 jit_solution(11503817156681811645)
XLA Ops:
  0.7 0.0 copy-start
  0.7 1.6 %copy-done = bf16[1,256,4096]{2,1,0:T(8,128)(2,1)S(1)} copy-done((bf16[1,256,4096]{2,1,0:T(8,128)(2,1)S(1)}, bf16[1,256,4096]{2,1,0:T(8,128)(2,1)}, u32[]{:S(2)}) %copy-start) | copy-done | bytes 2097176
  2.2 0.0 copy-start.1
  2.2 1.1 %copy-done.1 = bf16[1024,384]{1,0:T(8,128)(2,1)S(1)} copy-done((bf16[1024,384]{1,0:T(8,128)(2,1)S(1)}, bf16[1024,384]{1,0:T(8,128)(2,1)}, u32[]{:S(2)}) %copy-start.1) | copy-done | bytes 786456
  3.4 0.0 copy-start.2
  3.4 0.7 %copy-done.2 = s32[1,32]{1,0:T(1,128)S(1)} copy-done((s32[1,32]{1,0:T(1,128)S(1)}, s32[1,32]{1,0:T(1,128)}, u32[]{:S(2)}) %copy-start.2) | copy-done | bytes 152
  4.0 0.0 copy-start.3
  4.0 0.7 %copy-done.3 = s32[1,8]{1,0:T(1,128)S(1)} copy-done((s32[1,8]{1,0:T(1,128)S(1)}, s32[1,8]{1,0:T(1,128)}, u32[]{:S(2)}) %copy-start.3) | copy-done | bytes 56
  4.7 34.1 %shard_map.55 = bf16[1,256,128]{2,1,0:T(8,128)(2,1)S(1)} custom-call(bf16[1,256,4096]{2,1,0:T(8,128)(2,1)S(1)} %copy-done, s32[1,1]{1,0:T(1,128)S(6)} %copy.7.pad_ref, s32[1,32]{1,0:T(1,128)S(1)} %copy-done.2, s32[1,8]{1,0:T(1,128)S(1)} %copy-done.3, bf16[1024,384]{1,0:T(8,128)(2,1)S(1)} %copy-done.1), custom_call_target="tpu_custom_call" | custom-call | flops 603979776 | bytes 5242880 | tf_op jit(solution)/shard_map/pallas_call | solution.py:277
  38.8 0.6 %copy.8 = bf16[1,256,128]{2,1,0:T(8,128)(2,1)} copy(bf16[1,256,128]{2,1,0:T(8,128)(2,1)S(1)} %shard_map.55) | data formatting | bytes 131072
Async XLA Ops:
  0.7 1.6 %copy-start = (bf16[1,256,4096]{2,1,0:T(8,128)(2,1)S(1)}, bf16[1,256,4096]{2,1,0:T(8,128)(2,1)}, u32[]{:S(2)}) copy-start(bf16[1,256,4096]{2,1,0:T(8,128)(2,1)} %hidden_ref.1) | copy-start | bytes 6291460
  2.2 1.1 %copy-start.1 = (bf16[1024,384]{1,0:T(8,128)(2,1)S(1)}, bf16[1024,384]{1,0:T(8,128)(2,1)}, u32[]{:S(2)}) copy-start(bf16[1024,384]{1,0:T(8,128)(2,1)} %weight_ref.1) | copy-start | bytes 2359300
  3.4 0.7 %copy-start.2 = (s32[1,32]{1,0:T(1,128)S(1)}, s32[1,32]{1,0:T(1,128)}, u32[]{:S(2)}) copy-start(s32[1,32]{1,0:T(1,128)} %docs_ref.1) | copy-start | bytes 388
  4.0 0.7 %copy-start.3 = (s32[1,8]{1,0:T(1,128)S(1)}, s32[1,8]{1,0:T(1,128)}, u32[]{:S(2)}) copy-start(s32[1,8]{1,0:T(1,128)} %shift_ref.1) | copy-start | bytes 100

commit v2 on v1

--- a/solution.py
+++ b/solution.py
@@ -20,6 +20,25 @@
     return out
 
 
+def flipped(index, bits):
+    out, bit = index, 1
+    while bit <= bits:
+        if bits & bit:
+            out = out + bit - 2 * bit * ((index // bit) % 2)
+        bit *= 2
+    return out
+
+
+def nearest_first(index, count):
+    both = jnp.minimum(index, count - 1 - index)
+    longer = jnp.where(index <= count - 1 - index, 1, -1)
+    out = []
+    for j in range(1, count):
+        near = (j + 1) // 2 if j % 2 else -(j // 2)
+        out.append(index + jnp.where(j <= 2 * both, near, longer * (j - both)))
+    return out
+
+
 def share_count(chips, depth):
     for shares in (4, 2):
         halves = 2 if shares == 4 else 1
@@ -33,11 +52,14 @@
     n_dp,
     shares,
     hidden_ref,
+    pad_hbm,
+    docs_hbm,
+    shift_hbm,
+    weight_ref,
+    out_ref,
     pad_ref,
     docs_ref,
     shift_ref,
-    weight_ref,
-    out_ref,
     rows_buf,
     weights,
     total,
@@ -71,7 +93,8 @@
     piece = depth // (2 * shares)
     over_x, over_y, over_xy = flipped(place, 1), flipped(place, 2), flipped(place, 3)
     x_peer, y_peer = flipped(sp, 2), flipped(sp, 4)
-    shards = [flipped(dp, j) for j in range(1, n_dp)]
+    shards = nearest_first(dp, n_dp)
+    inner = (dp > 0) & (dp < n_dp - 1)
     prior, later = (sp + n_sp - 1) % n_sp, (sp + 1) % n_sp
 
     def rows_of(which_core, which_place, half=None):
@@ -86,8 +109,12 @@
     fetch_rows.start()
     fetch_weight = pltpu.make_async_copy(weight_ref, weights.at[dp], local_sem.at[1])
     fetch_weight.start()
-    padding = pad_ref[0, 0]
-    pads[sp] = jnp.full(pads.shape[1:], padding, jnp.int32)
+    fetch_pad = pltpu.make_async_copy(pad_hbm, pad_ref, local_sem.at[2])
+    fetch_pad.start()
+    fetch_docs = pltpu.make_async_copy(docs_hbm, docs_ref, local_sem.at[3])
+    fetch_docs.start()
+    fetch_shift = pltpu.make_async_copy(shift_hbm, shift_ref, local_sem.at[4])
+    fetch_shift.start()
 
     barrier = pltpu.get_barrier_semaphore()
     for j in range(1, n_sp):
@@ -96,23 +123,28 @@
         )
     for j in range(1, n_dp):
         pl.semaphore_signal(
-            barrier, inc=1, device_id={"dp": shards[j - 1]}, device_id_type=MESH
+            barrier, inc=1, device_id={"dp": (dp + j) % n_dp}, device_id_type=MESH
         )
     pl.semaphore_wait(barrier, n_sp - 1 + n_dp - 1)
 
     started = []
 
-    def send(src, dst, send_sem, recv_sem, device):
-        copy = pltpu.make_async_remote_copy(
-            src_ref=src,
-            dst_ref=dst,
-            send_sem=send_sem,
-            recv_sem=recv_sem,
-            device_id=device,
-            device_id_type=MESH,
-        )
-        copy.start()
-        started.append(copy)
+    def send(src, dst, send_sem, recv_sem, device, when=None):
+        def copy():
+            return pltpu.make_async_remote_copy(
+                src_ref=src(),
+                dst_ref=dst(),
+                send_sem=send_sem,
+                recv_sem=recv_sem,
+                device_id=device,
+                device_id_type=MESH,
+            )
+
+        if when is None:
+            copy().start()
+        else:
+            pl.when(when)(lambda: copy().start())
+        started.append((copy, when))
 
     def arrived(dst, send_sem, recv_sem, device):
         pltpu.make_async_remote_copy(
@@ -125,42 +157,71 @@
         ).wait_recv()
 
     own = rows_of(core, place)
-    for j in range(n_dp - 1):
-        send(
-            weight_ref.at[own, :],
-            weights.at[dp, own, :],
-            z_send.at[j],
-            z_recv.at[j],
-            {"dp": shards[j]},
-        )
+    own_source = lambda: weight_ref.at[own, :]
+    own_target = lambda: weights.at[dp, own, :]
+    if n_dp > 1:
+        send(own_source, own_target, z_send.at[n_dp], z_recv.at[dp], {"dp": dp + 1}, when=dp < n_dp - 1)
+        send(own_source, own_target, z_send.at[n_dp + 1], z_recv.at[dp], {"dp": dp - 1}, when=dp > 0)
+    fetch_pad.wait()
+    padding = pad_ref[0, 0]
+    pads[sp] = jnp.full(pads.shape[1:], padding, jnp.int32)
     for j in range(1, n_sp):
-        send(pads.at[sp], pads.at[sp], pad_send.at[j - 1], pad_recv.at[j - 1], {"sp": (sp + j) % n_sp})
+        block = lambda: pads.at[sp]
+        send(block, block, pad_send.at[j - 1], pad_recv.at[j - 1], {"sp": (sp + j) % n_sp})
 
     def to_sibling(j, slot, rows):
-        block = weights.at[shards[j], rows, :]
+        block = lambda: weights.at[shards[j], rows, :]
         send(block, block, sib_send.at[j, slot], sib_recv.at[j, slot], {"sp": sibling})
 
+    def piece_copies(j):
+        shard = shards[j]
+        onward = jnp.where(shard < dp, dp + 1, dp - 1)
+        block = weights.at[shard, own, :]
+        ways = [
+            (z_send.at[shard], z_recv.at[shard], {"dp": onward}, (onward >= 0) & (onward < n_dp))
+        ]
+        if shares >= 2:
+            ways.append((plane_send.at[j, 0], plane_recv.at[j, 0], {"sp": x_peer}, None))
+        if shares >= 4:
+            ways.append((plane_send.at[j, 1], plane_recv.at[j, 1], {"sp": y_peer}, None))
+        ways.append((sib_send.at[j, 0], sib_recv.at[j, 0], {"sp": sibling}, None))
+        return [
+            (
+                lambda ways=(out, into, peer): pltpu.make_async_remote_copy(
+                    src_ref=block,
+                    dst_ref=block,
+                    send_sem=ways[0],
+                    recv_sem=ways[1],
+                    device_id=ways[2],
+                    device_id_type=MESH,
+                ),
+                when,
+            )
+            for out, into, peer, when in ways
+        ]
+
     def from_plane(j):
-        block = weights.at[shards[j], own, :]
-        arrived(block, z_send.at[j], z_recv.at[j], {"dp": shards[j]})
-        if shares >= 2:
-            send(block, block, plane_send.at[j, 0], plane_recv.at[j, 0], {"sp": x_peer})
-        if shares >= 4:
-            send(block, block, plane_send.at[j, 1], plane_recv.at[j, 1], {"sp": y_peer})
-        to_sibling(j, 0, own)
+        shard = shards[j]
+        origin = jnp.where(shard < dp, dp - 1, dp + 1)
+        arrived(weights.at[shard, own, :], z_send.at[shard], z_recv.at[shard], {"dp": origin})
+        for copy, when in piece_copies(j):
+            if when is None:
+                copy().start()
+            else:
+                pl.when(when)(lambda: copy().start())
 
     def from_neighbours(j):
         if shares >= 2:
             rows = rows_of(core, over_x)
             arrived(weights.at[shards[j], rows, :], plane_send.at[j, 0], plane_recv.at[j, 0], {"sp": x_peer})
             if shares >= 4:
-                block = weights.at[shards[j], rows_of(core, over_x, 0), :]
+                block = lambda: weights.at[shards[j], rows_of(core, over_x, 0), :]
                 send(block, block, diag_send.at[j, 0], diag_recv.at[j, 0], {"sp": y_peer})
             to_sibling(j, 1, rows)
         if shares >= 4:
             rows = rows_of(core, over_y)
             arrived(weights.at[shards[j], rows, :], plane_send.at[j, 1], plane_recv.at[j, 1], {"sp": y_peer})
-            block = weights.at[shards[j], rows_of(core, over_y, 1), :]
+            block = lambda: weights.at[shards[j], rows_of(core, over_y, 1), :]
             send(block, block, diag_send.at[j, 1], diag_recv.at[j, 1], {"sp": x_peer})
             to_sibling(j, 2, rows)
 
@@ -187,11 +248,16 @@
         total[...] = product(dp)
 
     own_shard()
+    if n_dp > 1:
+        from_plane(0)
     for j in range(n_dp - 1):
-        from_plane(j)
+        if j < n_dp - 2:
+            pl.when(inner)(functools.partial(from_plane, j + 1))
+        from_neighbours(j)
         if j > 0:
             from_diagonal(j - 1)
-        from_neighbours(j)
+        if j < n_dp - 2:
+            pl.when(~inner)(functools.partial(from_plane, j + 1))
         if j > 0:
             from_sibling(j - 1)
             total[...] += product(shards[j - 1])
@@ -203,6 +269,8 @@
     for i in range(n_sp):
         before = before + jnp.where(i < sp, rows_dev - pads[i], 0)
     live = rows_dev - padding
+    fetch_docs.wait()
+    fetch_shift.wait()
     shift = jnp.where(sp == 0, 0, shift_ref[0, sp])
     next_shift = jnp.where(sp == n_sp - 1, 0, shift_ref[0, later])
     owned_count = live + next_shift - shift
@@ -243,9 +311,9 @@
     own_rows = pl.ds(2 * edge, slots)
     cand[own_rows, :] = projected
     tail = cand.at[pl.ds(rows_dev - edge, edge), :]
-    send(tail, cand.at[pl.ds(0, edge), :], edge_send.at[0], edge_recv.at[0], {"sp": later})
+    send(lambda: tail, lambda: cand.at[pl.ds(0, edge), :], edge_send.at[0], edge_recv.at[0], {"sp": later})
     head[...] = jnp.dot(head_pick, projected, preferred_element_type=jnp.float32).astype(jnp.bfloat16)
-    send(head, cand.at[pl.ds(edge, edge), :], edge_send.at[1], edge_recv.at[1], {"sp": prior})
+    send(lambda: head, lambda: cand.at[pl.ds(edge, edge), :], edge_send.at[1], edge_recv.at[1], {"sp": prior})
     arrived(cand.at[pl.ds(0, edge), :], edge_send.at[0], edge_recv.at[0], {"sp": later})
     arrived(cand.at[pl.ds(edge, edge), :], edge_send.at[1], edge_recv.at[1], {"sp": prior})
 
@@ -260,8 +328,13 @@
     probs = (exponent / jnp.sum(exponent, axis=1, keepdims=True)).astype(jnp.bfloat16)
     result = jnp.dot(probs, values, preferred_element_type=jnp.float32)
     out_ref[0] = jnp.where(query_live, result, 0.0).astype(out_ref.dtype)
-    for copy in started:
-        copy.wait_send()
+    for j in range(n_dp - 1):
+        started.extend(piece_copies(j))
+    for copy, when in started:
+        if when is None:
+            copy().wait_send()
+        else:
+            pl.when(when)(lambda: copy().wait_send())
 
 
 def solution(mesh):
@@ -278,23 +351,23 @@
             functools.partial(kernel, n_sp, n_dp, shares),
             out_shape=jax.ShapeDtypeStruct((1, rows_dev, columns // 3), hidden.dtype),
             in_specs=[
-                pl.BlockSpec(memory_space=pl.ANY),
-                pl.BlockSpec(memory_space=pltpu.SMEM),
-                pl.BlockSpec(memory_space=pltpu.VMEM),
-                pl.BlockSpec(memory_space=pltpu.SMEM),
-                pl.BlockSpec(memory_space=pl.ANY),
-            ],
+                pl.BlockSpec(memory_space=pltpu.HBM),
+            ]
+            * 5,
             out_specs=pl.BlockSpec(memory_space=pltpu.VMEM),
             scratch_shapes=[
+                pltpu.SMEM(pad_counts.shape, jnp.int32),
+                pltpu.VMEM(doc_lengths.shape, jnp.int32),
+                pltpu.SMEM(range_shift.shape, jnp.int32),
                 pltpu.VMEM((slots, width), hidden.dtype),
                 pltpu.VMEM((n_dp, depth, columns), qkv_weight.dtype),
                 pltpu.VMEM((slots, columns), jnp.float32),
                 pltpu.VMEM((n_sp, 8, 128), jnp.int32),
                 pltpu.VMEM((rows_dev, columns), hidden.dtype),
                 pltpu.VMEM((edge, columns), hidden.dtype),
-                dma((2,)),
-                dma((others,)),
-                dma((others,)),
+                dma((5,)),
+                dma((n_dp + 2,)),
+                dma((n_dp,)),
                 dma((others, 2)),
                 dma((others, 2)),
                 dma((others, 2)),
@@ -307,7 +380,7 @@
                 dma((2,)),
             ],
             compiler_params=pltpu.CompilerParams(
-                collective_id=0, has_side_effects=True, vmem_limit_bytes=48 * 1024 * 1024
+                collective_id=0, has_side_effects=True, vmem_limit_bytes=63 * 1024 * 1024
             ),
             cost_estimate=pl.CostEstimate(
                 flops=2 * slots * width * columns,

time: 39.7 us -> 35.9 us (0.904)
  local copies, waits for them, and re-layouts: 4.66 us -> 1.47 us
  Pallas kernels: 34.1 us -> 33.6 us
    unnamed x9 -> x1, local copies, waits for them, and re-layouts: 4.66 us -> 1.47 us
    pallas_call x1, Pallas kernels: 34.1 us -> 33.6 us  [step(): pl.pallas_call(functools.partial(kernel, n_sp, n_dp, shares), out_shape=j...]
where the time goes in v2:
time: 35.9 us; the launch traced here: 35.8 us
  Pallas kernels  33.6 us (94%)
  local copies, waits for them, and re-layouts  1.47 us (4%)
  between operations  0.66 us (2%)
    pallas_call x1, Pallas kernels, step(): pl.pallas_call(functools.partial(kernel, n_sp, n_dp, shares), out_shape=j...  33.6 us
    unnamed x1, local copies, waits for them, and re-layouts  1.47 us

profile of v2, /device:TPU:0, one launch (start us, length us, event | category | flops | bytes accessed | tf_op | source)
XLA Modules:
  0.0 35.8 jit_solution(6779957329363292934)
XLA Ops:
  0.7 33.6 %shard_map.55 = bf16[1,256,128]{2,1,0:T(8,128)(2,1)} custom-call(bf16[1,256,4096]{2,1,0:T(8,128)(2,1)} %hidden_ref.1, s32[1,1]{1,0:T(1,128)S(6)} %copy.7.pad_hbm, s32[1,32]{1,0:T(1,128)} %docs_hbm.1, s32[1,8]{1,0:T(1,128)} %shift_hbm.1, bf16[1024,384]{1,0:T(8,128)(2,1)} %weight_ref.1), custom_call_target="tpu_custom_call" | custom-call | flops 603979776 | bytes 5242880 | tf_op jit(solution)/shard_map/pallas_call | solution.py:350
  34.3 1.5 %copy.8 = bf16[1,256,128]{2,1,0:T(8,128)(2,1)} copy(bf16[1,256,128]{2,1,0:T(8,128)(2,1)} %shard_map.55) | data formatting | bytes 131072

commit v3 on v2

--- a/solution.py
+++ b/solution.py
@@ -9,6 +9,7 @@
 from jax.sharding import PartitionSpec as P
 
 MESH = pl.DeviceIdType.MESH
+PARTS = 2
 
 
 def flipped(index, bits):
@@ -36,6 +37,21 @@
     for j in range(1, count):
         near = (j + 1) // 2 if j % 2 else -(j // 2)
         out.append(index + jnp.where(j <= 2 * both, near, longer * (j - both)))
+    return out
+
+
+def travel_order(index, count, parts):
+    near = nearest_first(index, count)
+    both = jnp.minimum(index, count - 1 - index)
+    out = []
+    for pair in range(0, count - 1, 2):
+        if pair + 1 == count - 1:
+            out += [(near[pair], part) for part in range(parts)]
+            continue
+        two_sided = pair // 2 < both
+        for step in range(2 * parts):
+            shard = jnp.where(two_sided, near[pair + step % 2], near[pair + step // parts])
+            out.append((shard, jnp.where(two_sided, step // 2, step % parts)))
     return out
 
 
@@ -90,10 +106,14 @@
     core = sp % 2
     place = (sp // 2) % shares
     sibling = flipped(sp, 1)
-    piece = depth // (2 * shares)
+    part_depth = depth // PARTS
+    piece = part_depth // (2 * shares)
     over_x, over_y, over_xy = flipped(place, 1), flipped(place, 2), flipped(place, 3)
     x_peer, y_peer = flipped(sp, 2), flipped(sp, 4)
-    shards = nearest_first(dp, n_dp)
+    units = travel_order(dp, n_dp, PARTS)
+    origins = [shard for shard, _ in units]
+    shards = [shard * PARTS + part for shard, part in units]
+    n_units = len(units)
     inner = (dp > 0) & (dp < n_dp - 1)
     prior, later = (sp + n_sp - 1) % n_sp, (sp + 1) % n_sp
 
@@ -107,8 +127,16 @@
         hidden_ref.at[0, pl.ds(least_pad, slots), :], rows_buf, local_sem.at[0]
     )
     fetch_rows.start()
-    fetch_weight = pltpu.make_async_copy(weight_ref, weights.at[dp], local_sem.at[1])
-    fetch_weight.start()
+    fetch_weights = [
+        pltpu.make_async_copy(
+            weight_ref.at[pl.ds(part * part_depth, part_depth), :],
+            weights.at[dp * PARTS + part],
+            local_sem.at[5 + part],
+        )
+        for part in range(PARTS)
+    ]
+    for fetch in fetch_weights:
+        fetch.start()
     fetch_pad = pltpu.make_async_copy(pad_hbm, pad_ref, local_sem.at[2])
     fetch_pad.start()
     fetch_docs = pltpu.make_async_copy(docs_hbm, docs_ref, local_sem.at[3])
@@ -157,11 +185,14 @@
         ).wait_recv()
 
     own = rows_of(core, place)
-    own_source = lambda: weight_ref.at[own, :]
-    own_target = lambda: weights.at[dp, own, :]
-    if n_dp > 1:
-        send(own_source, own_target, z_send.at[n_dp], z_recv.at[dp], {"dp": dp + 1}, when=dp < n_dp - 1)
-        send(own_source, own_target, z_send.at[n_dp + 1], z_recv.at[dp], {"dp": dp - 1}, when=dp > 0)
+    for part in range(PARTS if n_dp > 1 else 0):
+        mine = dp * PARTS + part
+        start = part * part_depth + (core * shares + place) * piece
+        own_source = lambda start=start: weight_ref.at[pl.ds(pl.multiple_of(start, 16), piece), :]
+        own_target = lambda mine=mine: weights.at[mine, own, :]
+        at = n_dp * PARTS + 2 * part
+        send(own_source, own_target, z_send.at[at], z_recv.at[mine], {"dp": dp + 1}, dp < n_dp - 1)
+        send(own_source, own_target, z_send.at[at + 1], z_recv.at[mine], {"dp": dp - 1}, dp > 0)
     fetch_pad.wait()
     padding = pad_ref[0, 0]
     pads[sp] = jnp.full(pads.shape[1:], padding, jnp.int32)
@@ -175,7 +206,7 @@
 
     def piece_copies(j):
         shard = shards[j]
-        onward = jnp.where(shard < dp, dp + 1, dp - 1)
+        onward = jnp.where(origins[j] < dp, dp + 1, dp - 1)
         block = weights.at[shard, own, :]
         ways = [
             (z_send.at[shard], z_recv.at[shard], {"dp": onward}, (onward >= 0) & (onward < n_dp))
@@ -202,7 +233,7 @@
 
     def from_plane(j):
         shard = shards[j]
-        origin = jnp.where(shard < dp, dp - 1, dp + 1)
+        origin = jnp.where(origins[j] < dp, dp - 1, dp + 1)
         arrived(weights.at[shard, own, :], z_send.at[shard], z_recv.at[shard], {"dp": origin})
         for copy, when in piece_copies(j):
             if when is None:
@@ -238,29 +269,33 @@
             block = weights.at[shards[j], rows_of(1 - core, which), :]
             arrived(block, sib_send.at[j, slot], sib_recv.at[j, slot], {"sp": sibling})
 
-    def product(shard):
-        part = pl.ds(pl.multiple_of(shard * depth, 128), depth)
-        return jnp.dot(rows_buf[:, part], weights[shard], preferred_element_type=jnp.float32)
-
-    def own_shard():
-        fetch_rows.wait()
-        fetch_weight.wait()
-        total[...] = product(dp)
-
-    own_shard()
-    if n_dp > 1:
-        from_plane(0)
-    for j in range(n_dp - 1):
-        if j < n_dp - 2:
-            pl.when(inner)(functools.partial(from_plane, j + 1))
-        from_neighbours(j)
-        if j > 0:
-            from_diagonal(j - 1)
-        if j < n_dp - 2:
-            pl.when(~inner)(functools.partial(from_plane, j + 1))
-        if j > 0:
-            from_sibling(j - 1)
-            total[...] += product(shards[j - 1])
+    def product(unit):
+        part = pl.ds(pl.multiple_of(unit * part_depth, 128), part_depth)
+        return jnp.dot(rows_buf[:, part], weights[unit], preferred_element_type=jnp.float32)
+
+    fetch_rows.wait()
+    for fetch in fetch_weights:
+        fetch.wait()
+    total[...] = product(dp * PARTS)
+    for part in range(1, PARTS):
+        total[...] += product(dp * PARTS + part)
+    for i in range(4):
+        if i < n_units:
+            if i < 2:
+                from_plane(i)
+            else:
+                pl.when(inner)(functools.partial(from_plane, i))
+    for i in range(n_units):
+        from_neighbours(i)
+        if i + 4 < n_units:
+            pl.when(inner)(functools.partial(from_plane, i + 4))
+        if i + 2 < n_units:
+            pl.when(~inner)(functools.partial(from_plane, i + 2))
+        if i >= 1:
+            from_diagonal(i - 1)
+        if i >= 2:
+            from_sibling(i - 2)
+            total[...] += product(shards[i - 2])
 
     for j in range(1, n_sp):
         block = pads.at[(sp + n_sp - j) % n_sp]
@@ -301,12 +336,13 @@
     head_pick = (head_col == head_row + padding - least_pad).astype(jnp.float32).astype(jnp.bfloat16)
     query_live = lax.broadcasted_iota(jnp.int32, (rows_dev, head_dim), 0) < owned_count
 
-    if n_dp > 1:
-        from_diagonal(n_dp - 2)
-        from_sibling(n_dp - 2)
-        projected = (total[...] + product(shards[n_dp - 2])).astype(jnp.bfloat16)
-    else:
-        projected = total[...].astype(jnp.bfloat16)
+    if n_units:
+        from_diagonal(n_units - 1)
+        from_sibling(n_units - 2)
+        total[...] += product(shards[n_units - 2])
+        from_sibling(n_units - 1)
+        total[...] += product(shards[n_units - 1])
+    projected = total[...].astype(jnp.bfloat16)
 
     own_rows = pl.ds(2 * edge, slots)
     cand[own_rows, :] = projected
@@ -328,7 +364,7 @@
     probs = (exponent / jnp.sum(exponent, axis=1, keepdims=True)).astype(jnp.bfloat16)
     result = jnp.dot(probs, values, preferred_element_type=jnp.float32)
     out_ref[0] = jnp.where(query_live, result, 0.0).astype(out_ref.dtype)
-    for j in range(n_dp - 1):
+    for j in range(n_units):
         started.extend(piece_copies(j))
     for copy, when in started:
         if when is None:
@@ -343,9 +379,9 @@
     def step(hidden, pad_counts, doc_lengths, range_shift, qkv_weight):
         rows_dev, width = hidden.shape[1:]
         depth, columns = qkv_weight.shape
-        shares = share_count(n_sp // 2, depth)
+        shares = share_count(n_sp // 2, depth // PARTS)
         edge, slots = rows_dev // 8, rows_dev - rows_dev // 4
-        others = max(n_dp - 1, 1)
+        others = max(n_dp - 1, 1) * PARTS
         dma = pltpu.SemaphoreType.DMA
         return pl.pallas_call(
             functools.partial(kernel, n_sp, n_dp, shares),
@@ -360,14 +396,14 @@
                 pltpu.VMEM(doc_lengths.shape, jnp.int32),
                 pltpu.SMEM(range_shift.shape, jnp.int32),
                 pltpu.VMEM((slots, width), hidden.dtype),
-                pltpu.VMEM((n_dp, depth, columns), qkv_weight.dtype),
+                pltpu.VMEM((n_dp * PARTS, depth // PARTS, columns), qkv_weight.dtype),
                 pltpu.VMEM((slots, columns), jnp.float32),
                 pltpu.VMEM((n_sp, 8, 128), jnp.int32),
                 pltpu.VMEM((rows_dev, columns), hidden.dtype),
                 pltpu.VMEM((edge, columns), hidden.dtype),
-                dma((5,)),
-                dma((n_dp + 2,)),
-                dma((n_dp,)),
+                dma((5 + PARTS,)),
+                dma(((n_dp + 2) * PARTS,)),
+                dma((n_dp * PARTS,)),
                 dma((others, 2)),
                 dma((others, 2)),
                 dma((others, 2)),

time: 35.9 us -> 33.5 us (0.933)
  Pallas kernels: 33.6 us -> 31.2 us
    pallas_call x1, Pallas kernels: 33.6 us -> 31.2 us  [step(): pl.pallas_call(functools.partial(kernel, n_sp, n_dp, shares), out_shape=j...]
where the time goes in v3:
time: 33.5 us; the launch traced here: 33.3 us
  Pallas kernels  31.2 us (93%)
  local copies, waits for them, and re-layouts  1.47 us (4%)
  between operations  0.66 us (2%)
    pallas_call x1, Pallas kernels, step(): pl.pallas_call(functools.partial(kernel, n_sp, n_dp, shares), out_shape=j...  31.2 us
    unnamed x1, local copies, waits for them, and re-layouts  1.47 us

profile of v3, /device:TPU:0, one launch (start us, length us, event | category | flops | bytes accessed | tf_op | source)
XLA Modules:
  0.0 33.3 jit_solution(15052156323829323543)
XLA Ops:
  0.7 31.2 %shard_map.55 = bf16[1,256,128]{2,1,0:T(8,128)(2,1)} custom-call(bf16[1,256,4096]{2,1,0:T(8,128)(2,1)} %hidden_ref.1, s32[1,1]{1,0:T(1,128)S(6)} %copy.7.pad_hbm, s32[1,32]{1,0:T(1,128)} %docs_hbm.1, s32[1,8]{1,0:T(1,128)} %shift_hbm.1, bf16[1024,384]{1,0:T(8,128)(2,1)} %weight_ref.1), custom_call_target="tpu_custom_call" | custom-call | flops 603979776 | bytes 5242880 | tf_op jit(solution)/shard_map/pallas_call | solution.py:386
  31.9 1.5 %copy.8 = bf16[1,256,128]{2,1,0:T(8,128)(2,1)} copy(bf16[1,256,128]{2,1,0:T(8,128)(2,1)} %shard_map.55) | data formatting | bytes 131072

commit v4 on v3

--- a/solution.py
+++ b/solution.py
@@ -123,6 +123,10 @@
             return pl.ds(pl.multiple_of(start, 16), piece)
         return pl.ds(pl.multiple_of(start + half * (piece // 2), 16), piece // 2)
 
+    def half_of(which_core):
+        half = part_depth // 2
+        return pl.ds(pl.multiple_of(which_core * half, 16), half)
+
     fetch_rows = pltpu.make_async_copy(
         hidden_ref.at[0, pl.ds(least_pad, slots), :], rows_buf, local_sem.at[0]
     )
@@ -215,7 +219,8 @@
             ways.append((plane_send.at[j, 0], plane_recv.at[j, 0], {"sp": x_peer}, None))
         if shares >= 4:
             ways.append((plane_send.at[j, 1], plane_recv.at[j, 1], {"sp": y_peer}, None))
-        ways.append((sib_send.at[j, 0], sib_recv.at[j, 0], {"sp": sibling}, None))
+        if j == n_units - 1:
+            ways.append((sib_send.at[j, 0], sib_recv.at[j, 0], {"sp": sibling}, None))
         return [
             (
                 lambda ways=(out, into, peer): pltpu.make_async_remote_copy(
@@ -248,25 +253,32 @@
             if shares >= 4:
                 block = lambda: weights.at[shards[j], rows_of(core, over_x, 0), :]
                 send(block, block, diag_send.at[j, 0], diag_recv.at[j, 0], {"sp": y_peer})
-            to_sibling(j, 1, rows)
+            if j == n_units - 1:
+                to_sibling(j, 1, rows)
         if shares >= 4:
             rows = rows_of(core, over_y)
             arrived(weights.at[shards[j], rows, :], plane_send.at[j, 1], plane_recv.at[j, 1], {"sp": y_peer})
             block = lambda: weights.at[shards[j], rows_of(core, over_y, 1), :]
             send(block, block, diag_send.at[j, 1], diag_recv.at[j, 1], {"sp": x_peer})
-            to_sibling(j, 2, rows)
+            if j == n_units - 1:
+                to_sibling(j, 2, rows)
 
     def from_diagonal(j):
         if shares >= 4:
             for half, peer in ((0, y_peer), (1, x_peer)):
                 block = weights.at[shards[j], rows_of(core, over_xy, half), :]
                 arrived(block, diag_send.at[j, half], diag_recv.at[j, half], {"sp": peer})
+        if j < n_units - 1:
+            to_sibling(j, 0, half_of(core))
+        elif shares >= 4:
             to_sibling(j, 3, rows_of(core, over_xy))
 
     def from_sibling(j):
-        places = [place, over_x, over_y, over_xy][:shares]
-        for slot, which in enumerate(places):
-            block = weights.at[shards[j], rows_of(1 - core, which), :]
+        blocks = [half_of(1 - core)]
+        if j == n_units - 1:
+            blocks = [rows_of(1 - core, which) for which in (place, over_x, over_y, over_xy)[:shares]]
+        for slot, rows in enumerate(blocks):
+            block = weights.at[shards[j], rows, :]
             arrived(block, sib_send.at[j, slot], sib_recv.at[j, slot], {"sp": sibling})
 
     def product(unit):
@@ -350,6 +362,15 @@
     send(lambda: tail, lambda: cand.at[pl.ds(0, edge), :], edge_send.at[0], edge_recv.at[0], {"sp": later})
     head[...] = jnp.dot(head_pick, projected, preferred_element_type=jnp.float32).astype(jnp.bfloat16)
     send(lambda: head, lambda: cand.at[pl.ds(edge, edge), :], edge_send.at[1], edge_recv.at[1], {"sp": prior})
+    sent_edges = [copy for copy, _ in started[-2:]]
+    del started[-2:]
+    for j in range(n_units):
+        started.extend(piece_copies(j))
+    for copy, when in started:
+        if when is None:
+            copy().wait_send()
+        else:
+            pl.when(when)(lambda: copy().wait_send())
     arrived(cand.at[pl.ds(0, edge), :], edge_send.at[0], edge_recv.at[0], {"sp": later})
     arrived(cand.at[pl.ds(edge, edge), :], edge_send.at[1], edge_recv.at[1], {"sp": prior})
 
@@ -364,13 +385,8 @@
     probs = (exponent / jnp.sum(exponent, axis=1, keepdims=True)).astype(jnp.bfloat16)
     result = jnp.dot(probs, values, preferred_element_type=jnp.float32)
     out_ref[0] = jnp.where(query_live, result, 0.0).astype(out_ref.dtype)
-    for j in range(n_units):
-        started.extend(piece_copies(j))
-    for copy, when in started:
-        if when is None:
-            copy().wait_send()
-        else:
-            pl.when(when)(lambda: copy().wait_send())
+    sent_edges[0]().wait_send()
+    sent_edges[1]().wait_send()
 
 
 def solution(mesh):

time: 33.5 us -> 33.6 us (level)
  no operation moved by 1% of the time
where the time goes in v4:
time: 33.6 us; the launch traced here: 33.4 us
  Pallas kernels  31.3 us (93%)
  local copies, waits for them, and re-layouts  1.47 us (4%)
  between operations  0.66 us (2%)
    pallas_call x1, Pallas kernels, step(): pl.pallas_call(functools.partial(kernel, n_sp, n_dp, shares), out_shape=j...  31.3 us
    unnamed x1, local copies, waits for them, and re-layouts  1.47 us

profile of v4, /device:TPU:0, one launch (start us, length us, event | category | flops | bytes accessed | tf_op | source)
XLA Modules:
  0.0 33.4 jit_solution(2943357828635159048)
XLA Ops:
  0.7 31.3 %shard_map.55 = bf16[1,256,128]{2,1,0:T(8,128)(2,1)} custom-call(bf16[1,256,4096]{2,1,0:T(8,128)(2,1)} %hidden_ref.1, s32[1,1]{1,0:T(1,128)S(6)} %copy.7.pad_hbm, s32[1,32]{1,0:T(1,128)} %docs_hbm.1, s32[1,8]{1,0:T(1,128)} %shift_hbm.1, bf16[1024,384]{1,0:T(8,128)(2,1)} %weight_ref.1), custom_call_target="tpu_custom_call" | custom-call | flops 603979776 | bytes 5242880 | tf_op jit(solution)/shard_map/pallas_call | solution.py:402
  32.0 1.5 %copy.8 = bf16[1,256,128]{2,1,0:T(8,128)(2,1)} copy(bf16[1,256,128]{2,1,0:T(8,128)(2,1)} %shard_map.55) | data formatting | bytes 131072

commit v5 on v4

--- a/solution.py
+++ b/solution.py
@@ -9,7 +9,7 @@
 from jax.sharding import PartitionSpec as P
 
 MESH = pl.DeviceIdType.MESH
-PARTS = 2
+PARTS = 4
 
 
 def flipped(index, bits):
@@ -291,18 +291,18 @@
     total[...] = product(dp * PARTS)
     for part in range(1, PARTS):
         total[...] += product(dp * PARTS + part)
-    for i in range(4):
+    for i in range(2 * PARTS):
         if i < n_units:
-            if i < 2:
+            if i < PARTS:
                 from_plane(i)
             else:
                 pl.when(inner)(functools.partial(from_plane, i))
     for i in range(n_units):
         from_neighbours(i)
-        if i + 4 < n_units:
-            pl.when(inner)(functools.partial(from_plane, i + 4))
-        if i + 2 < n_units:
-            pl.when(~inner)(functools.partial(from_plane, i + 2))
+        if i + 2 * PARTS < n_units:
+            pl.when(inner)(functools.partial(from_plane, i + 2 * PARTS))
+        if i + PARTS < n_units:
+            pl.when(~inner)(functools.partial(from_plane, i + PARTS))
         if i >= 1:
             from_diagonal(i - 1)
         if i >= 2:

time: 33.6 us -> 39.1 us (1.16)
  Pallas kernels: 31.3 us -> 36.8 us
    pallas_call x1, Pallas kernels: 31.3 us -> 36.8 us  [step(): pl.pallas_call(functools.partial(kernel, n_sp, n_dp, shares), out_shape=j...]
where the time goes in v5:
time: 39.1 us; the launch traced here: 39 us
  Pallas kernels  36.8 us (94%)
  local copies, waits for them, and re-layouts  1.47 us (4%)
  between operations  0.66 us (2%)
    pallas_call x1, Pallas kernels, step(): pl.pallas_call(functools.partial(kernel, n_sp, n_dp, shares), out_shape=j...  36.8 us
    unnamed x1, local copies, waits for them, and re-layouts  1.47 us

profile of v5, /device:TPU:0, one launch (start us, length us, event | category | flops | bytes accessed | tf_op | source)
XLA Modules:
  0.0 39.0 jit_solution(1415298270454694220)
XLA Ops:
  0.7 36.8 %shard_map.55 = bf16[1,256,128]{2,1,0:T(8,128)(2,1)} custom-call(bf16[1,256,4096]{2,1,0:T(8,128)(2,1)} %hidden_ref.1, s32[1,1]{1,0:T(1,128)S(6)} %copy.7.pad_hbm, s32[1,32]{1,0:T(1,128)} %docs_hbm.1, s32[1,8]{1,0:T(1,128)} %shift_hbm.1, bf16[1024,384]{1,0:T(8,128)(2,1)} %weight_ref.1), custom_call_target="tpu_custom_call" | custom-call | flops 603979776 | bytes 5242880 | tf_op jit(solution)/shard_map/pallas_call | solution.py:402
  37.5 1.5 %copy.8 = bf16[1,256,128]{2,1,0:T(8,128)(2,1)} copy(bf16[1,256,128]{2,1,0:T(8,128)(2,1)} %shard_map.55) | data formatting | bytes 131072

commit v6 on v4

--- a/solution.py
+++ b/solution.py
@@ -307,7 +307,8 @@
             from_diagonal(i - 1)
         if i >= 2:
             from_sibling(i - 2)
-            total[...] += product(shards[i - 2])
+            if i % 2:
+                total[...] += product(shards[i - 3]) + product(shards[i - 2])
 
     for j in range(1, n_sp):
         block = pads.at[(sp + n_sp - j) % n_sp]
@@ -351,9 +352,8 @@
     if n_units:
         from_diagonal(n_units - 1)
         from_sibling(n_units - 2)
-        total[...] += product(shards[n_units - 2])
         from_sibling(n_units - 1)
-        total[...] += product(shards[n_units - 1])
+        total[...] += product(shards[n_units - 2]) + product(shards[n_units - 1])
     projected = total[...].astype(jnp.bfloat16)
 
     own_rows = pl.ds(2 * edge, slots)

time: 33.6 us -> 33.4 us (level)
  no operation moved by 1% of the time
where the time goes in v6:
time: 33.4 us; the launch traced here: 33.2 us
  Pallas kernels  31.1 us (93%)
  local copies, waits for them, and re-layouts  1.47 us (4%)
  between operations  0.66 us (2%)
    pallas_call x1, Pallas kernels, step(): pl.pallas_call(functools.partial(kernel, n_sp, n_dp, shares), out_shape=j...  31.1 us
    unnamed x1, local copies, waits for them, and re-layouts  1.47 us

profile of v6, /device:TPU:0, one launch (start us, length us, event | category | flops | bytes accessed | tf_op | source)
XLA Modules:
  0.0 33.2 jit_solution(1553746324813062144)
XLA Ops:
  0.7 31.1 %shard_map.55 = bf16[1,256,128]{2,1,0:T(8,128)(2,1)} custom-call(bf16[1,256,4096]{2,1,0:T(8,128)(2,1)} %hidden_ref.1, s32[1,1]{1,0:T(1,128)S(6)} %copy.7.pad_hbm, s32[1,32]{1,0:T(1,128)} %docs_hbm.1, s32[1,8]{1,0:T(1,128)} %shift_hbm.1, bf16[1024,384]{1,0:T(8,128)(2,1)} %weight_ref.1), custom_call_target="tpu_custom_call" | custom-call | flops 603979776 | bytes 5242880 | tf_op jit(solution)/shard_map/pallas_call | solution.py:402
  31.7 1.5 %copy.8 = bf16[1,256,128]{2,1,0:T(8,128)(2,1)} copy(bf16[1,256,128]{2,1,0:T(8,128)(2,1)} %shard_map.55) | data formatting | bytes 131072
